TPU v7x, 32 devices: a whole 2x2x4 slice. The times are simulated.
32 devices in a mesh: gz: 4 (over z), gx: 2 (over y), gy: 4 (over x, core).
Axes of the slice: x: 2, y: 2, z: 4, core: 2. Of those that a mesh axis runs over, the one named last changes fastest.
Arguments:
- hydro_state: float32 [8, 32, 128, 512], P(None, 'gx', 'gy', 'gz'), may hold values from -0.5 to 2, as said below
- material_id: int32 [32, 128, 512], P('gx', 'gy', 'gz'), may hold values from 0 to 3
- block_mask: int32 [1, 4, 16], replicated, may hold values 0 or 1
Outputs:
- hydro_next: float32 [8, 32, 128, 512], P(None, 'gx', 'gy', 'gz')
Inputs may be any that keep to these rules, and one draw needn't show every extreme that they name: `hydro_state`: field 0 lies in 0.9 to 2.0, fields 1 to 3 in -0.5 to 0.5, field 4 in 0.25 to 1.5, fields 5 and 7 in 0 to 1, field 6 in 0 to 0.5.
All inputs are finite; a program needn't handle non-finite values. Where the computation divides by a largest or mean magnitude, that divisor is 1e-20 or more.
Results may differ from a plain program's by a relative error of at most 0.00011.
Values sent between devices are 32-bit elements; how exact they have to be, the bound alone decides.
A program may use at most 128 MiB of HBM per device.

v0:
```python
import functools

import jax
import jax.numpy as jnp
from jax import lax
from jax.experimental import pallas as pl
from jax.experimental.pallas import tpu as pltpu
from jax.sharding import PartitionSpec as P

B = 32
CYCLES = 2
AXES = ("gx", "gy", "gz")
HALVES = 2
PAD = 8
TILE = 32
MESH = pl.DeviceIdType.MESH

courant = 0.15
visc_quad = 2.0
visc_linear = 0.5
rest_density = (1.0, 1.25, 1.5, 1.8)
sound_base = (1.0, 0.8, 1.2, 0.9)
hugoniot_slope = (1.5, 1.4, 1.2, 1.6)
gruneisen = (2.0, 1.7, 1.6, 2.2)
stiffness = tuple(r * c * c for r, c in zip(rest_density, sound_base))

STRESS = ((0, 1, 2), (1, 3, 4), (2, 4, 5))
COUNT = (3, 3, 8)


def pick(is_one, is_two, is_three, table):
    return jnp.where(
        is_three, table[3], jnp.where(is_two, table[2], jnp.where(is_one, table[1], table[0]))
    )


def equation_of_state(density, inverse, energy, material):
    tests = (material == 1, material == 2, material == 3)
    rest_rho = pick(*tests, rest_density)
    sound_zero = pick(*tests, sound_base)
    slope = pick(*tests, hugoniot_slope)
    gamma = pick(*tests, gruneisen)
    stiff = pick(*tests, stiffness)
    strain = 1.0 - rest_rho * inverse
    climb = slope * jnp.maximum(strain, 0.0)
    hugoniot = stiff * strain * (1.0 + climb * (2.0 + 3.0 * climb))
    pressure = hugoniot * (1.0 - 0.5 * gamma * strain) + gamma * density * energy
    return pressure, sound_zero + sound_zero * climb


def kernel(
    sizes, mask_ref, state_hbm, material_hbm, out_ref,
    vel, stress, cons, scal, inv, mat, pres, sound, terms,
    ys0, ys1, ys2, yr0, yr1, yr2, zs, zr, zc, peak, step,
    load_sem, send_sem, recv_sem, peak_send, peak_recv,
):
    _, nx, ny, nz = state_hbm.shape
    half = nx // HALVES
    index = {axis: lax.axis_index(axis) for axis in AXES}
    above = {axis: index[axis] < sizes[axis] - 1 for axis in AXES}
    below = {axis: index[axis] > 0 for axis in AXES}
    ys, yr = (ys0, ys1, ys2), (yr0, yr1, yr2)
    buffers = (vel, stress, cons)
    inner = pl.ds(PAD, ny)

    loads = [
        pltpu.make_async_copy(state_hbm.at[1:4], vel.at[0, :, 1 : nx + 1, PAD : PAD + ny], load_sem.at[0]),
        pltpu.make_async_copy(state_hbm.at[0:1], scal.at[0:1], load_sem.at[1]),
        pltpu.make_async_copy(state_hbm.at[4:8], scal.at[1:5], load_sem.at[2]),
        pltpu.make_async_copy(material_hbm, mat, load_sem.at[3]),
    ]
    for load in loads:
        load.start()

    barrier = pltpu.get_barrier_semaphore()
    total = 0
    for axis in AXES:
        for away in range(1, sizes[axis]):
            peer = lax.rem(index[axis] + away, sizes[axis])
            pl.semaphore_signal(barrier, inc=1, device_id={axis: peer}, device_id_type=MESH)
            total += 1

    for axis_number, axis in enumerate(AXES):
        for side, exists in ((0, below[axis]), (1, above[axis])):

            @pl.when(jnp.logical_not(exists))
            def _(axis_number=axis_number, side=side):
                for cycle in range(CYCLES):
                    for r in range(3):
                        if axis_number == 0:
                            ghost = (nx + 1) * side
                            for f in range(COUNT[r]):
                                buffers[r][cycle, f, ghost, inner, :] = jnp.zeros((ny, nz), jnp.float32)
                        elif axis_number == 1:
                            yr[r][cycle, side] = jnp.zeros(yr[r].shape[2:], jnp.float32)
                        else:
                            zr[cycle, r, :, side] = jnp.zeros((HALVES, ny, nz), jnp.float32)

    zs[...] = jnp.zeros_like(zs)
    for cycle in range(CYCLES):
        peak[cycle, 0, 0] = jnp.zeros((8, nz), jnp.float32)

    def copy(cycle, r, slot, side, src, dst, axis):
        move = 1 if side == 0 else sizes[axis] - 1
        return pltpu.make_async_remote_copy(
            src_ref=src,
            dst_ref=dst,
            send_sem=send_sem.at[cycle, r, slot],
            recv_sem=recv_sem.at[cycle, r, slot],
            device_id={axis: lax.rem(index[axis] + move, sizes[axis])},
            device_id_type=MESH,
        )

    def x_copy(cycle, r, side):
        own, ghost = (nx, 0) if side == 0 else (1, nx + 1)
        part = buffers[r].at[cycle, 0 : COUNT[r]]
        return copy(
            cycle, r, side, side,
            part.at[:, own, PAD : PAD + ny], part.at[:, ghost, PAD : PAD + ny], "gx",
        )

    def y_copy(cycle, r, h, side):
        rows = slice(h * half, (h + 1) * half)
        return copy(
            cycle, r, 2 + 4 * h + side, side,
            ys[r].at[cycle, side, :, rows], yr[r].at[cycle, side, :, rows], "gy",
        )

    def z_copy(cycle, r, h, side):
        return copy(
            cycle, r, 4 + 4 * h + side, side, zs.at[cycle, r, h], zr.at[cycle, r, h, side], "gz"
        )

    def for_side(exists, axis, act):
        if sizes[axis] > 1:
            pl.when(exists)(act)

    def send(cycle, r, h):
        side = 1 - h
        for_side((above if side == 0 else below)["gx"], "gx", lambda: x_copy(cycle, r, side).start())
        for s in range(2):
            way = above if s == 0 else below
            for_side(way["gy"], "gy", lambda: y_copy(cycle, r, h, s).start())
            for_side(way["gz"], "gz", lambda: z_copy(cycle, r, h, s).start())

    lane = lax.broadcasted_iota(jnp.int32, (TILE, nz), 1)
    first_lane, last_lane = lane == 0, lane == nz - 1
    pair = lane // 2

    def receive(cycle, r, h):
        for_side((below if h == 0 else above)["gx"], "gx", lambda: x_copy(cycle, r, h).wait_recv())
        for s in range(2):
            way = below if s == 0 else above
            for_side(way["gy"], "gy", lambda: y_copy(cycle, r, h, s).wait_recv())
            for_side(way["gz"], "gz", lambda: z_copy(cycle, r, h, s).wait_recv())
        fields = STRESS[1] if r == 1 else range(COUNT[r])

        def spread(i, carry):
            x = h * half + i
            for n, f in enumerate(fields):
                buffers[r][cycle, f, x + 1, pl.ds(PAD - 1, 1), :] = yr[r][cycle, 0, n, pl.ds(x, 1), :]
                buffers[r][cycle, f, x + 1, pl.ds(PAD + ny, 1), :] = yr[r][cycle, 1, n, pl.ds(x, 1), :]
            return carry

        lax.fori_loop(0, half, spread, 0)
        odd = lax.broadcasted_iota(jnp.int32, (ny, nz), 1) % 2 == 1
        zc[cycle, r, h] = jnp.where(
            odd, pltpu.roll(zr[cycle, r, h, 0], 1, 1), pltpu.roll(zr[cycle, r, h, 1], nz - 1, 1)
        )

    def pack(cycle, r, h, x, y0, values):
        rows = pl.ds(y0, TILE)
        edge = zs[cycle, r, h, rows, :]
        for n, value in enumerate(values):
            slot = (x - h * half) * len(values) + n
            edge = jnp.where(pair == slot, pltpu.roll(value, 2 * slot + 1, 1), edge)
        zs[cycle, r, h, rows, :] = edge

    def pack_rows(cycle, r, x, y0, values):
        for n, value in enumerate(values):
            if y0 + TILE == ny:
                ys[r][cycle, 0, n, pl.ds(x, 1), :] = value[TILE - 1 : TILE]
            if y0 == 0:
                ys[r][cycle, 1, n, pl.ds(x, 1), :] = value[0:1]

    def at(r, cycle, f, x, y0, dx=0, dy=0):
        return buffers[r][cycle, f, x + 1 + dx, pl.ds(PAD + y0 + dy, TILE), :]

    def z_pair(cycle, r, h, x, y0, n, value):
        slot = (x - h * half) * COUNT[r] + n
        ghost = pltpu.roll(zc[cycle, r, h, pl.ds(y0, TILE), :], nz - 1 - 2 * slot, 1)
        ahead = jnp.where(last_lane, ghost, pltpu.roll(value, nz - 1, 1))
        behind = jnp.where(first_lane, ghost, pltpu.roll(value, 1, 1))
        return ahead, behind

    def planes(h, body):
        def run(i, carry):
            x = h * half + i
            for y0 in range(0, ny, TILE):
                body(h, x, y0)
            return carry

        lax.fori_loop(0, half, run, 0)

    def begin(cycle, h, x, y0, density, inverse, energy, velocity):
        rows = pl.ds(y0, TILE)
        pressure, speed = equation_of_state(density, inverse, energy, mat[x, rows, :])
        pres[x, rows, :] = pressure
        sound[x, rows, :] = speed
        fast = speed + jnp.abs(velocity[0]) + jnp.abs(velocity[1]) + jnp.abs(velocity[2])
        top = peak[cycle, 0, 0]
        for r0 in range(0, TILE, 8):
            top = jnp.maximum(top, fast[r0 : r0 + 8])
        peak[cycle, 0, 0] = top
        pack(cycle, 0, h, x, y0, velocity)
        pack_rows(cycle, 0, x, y0, velocity)

    def stage_start(h, x, y0):
        rows = pl.ds(y0, TILE)
        density = scal[0, x, rows, :]
        inverse = 1.0 / density
        inv[x, rows, :] = inverse
        begin(0, h, x, y0, density, inverse, scal[1, x, rows, :], [at(0, 0, f, x, y0) for f in range(3)])

    def stage_stress(cycle, h, x, y0):
        rows = pl.ds(y0, TILE)
        g = []
        for f in range(3):
            ahead, behind = z_pair(cycle, 0, h, x, y0, f, at(0, cycle, f, x, y0))
            g.append((
                at(0, cycle, f, x, y0, dx=1) - at(0, cycle, f, x, y0, dx=-1),
                at(0, cycle, f, x, y0, dy=1) - at(0, cycle, f, x, y0, dy=-1),
                ahead - behind,
            ))
        div = 0.5 * (g[0][0] + g[1][1] + g[2][2])
        sxy, sxz, syz = g[0][1] + g[1][0], g[0][2] + g[2][0], g[1][2] + g[2][1]
        squares = 0.25 * (
            g[0][0] * g[0][0] + g[1][1] * g[1][1] + g[2][2] * g[2][2]
            + 0.5 * (sxy * sxy + sxz * sxz + syz * syz)
        )
        pressure = pres[x, rows, :]
        squash = jnp.maximum(-div, 0.0)
        mu = scal[0, x, rows, :] * squash * (visc_quad * squash + visc_linear * sound[x, rows, :])
        whole, quarter = 0.5 * mu, 0.25 * mu
        values = (
            whole * g[0][0] - pressure, quarter * sxy, quarter * sxz,
            whole * g[1][1] - pressure, quarter * syz, whole * g[2][2] - pressure,
        )
        for f, value in enumerate(values):
            stress[cycle, f, x + 1, pl.ds(PAD + y0, TILE), :] = value
        heat = mu * squares
        terms[0, x, rows, :] = div
        terms[1, x, rows, :] = heat - pressure * div
        terms[2, x, rows, :] = heat
        pack(cycle, 1, h, x, y0, [values[f] for f in STRESS[2]])
        pack_rows(cycle, 1, x, y0, [values[f] for f in STRESS[1]])

    def stage_conserved(cycle, h, x, y0):
        rows = pl.ds(y0, TILE)
        dt = step[0:1, :]
        inverse = inv[x, rows, :]
        scaled = dt * inverse
        density = scal[0, x, rows, :] / (1.0 + dt * terms[0, x, rows, :])
        values = [density]
        for i in range(3):
            fx, fy, fz = STRESS[i]
            ahead, behind = z_pair(cycle, 1, h, x, y0, i, at(1, cycle, fz, x, y0))
            force = (
                (at(1, cycle, fx, x, y0, dx=1) - at(1, cycle, fx, x, y0, dx=-1))
                + (at(1, cycle, fy, x, y0, dy=1) - at(1, cycle, fy, x, y0, dy=-1))
                + (ahead - behind)
            )
            values.append(density * (at(0, cycle, i, x, y0) + (0.5 * scaled) * force))
        values.append(density * (scal[1, x, rows, :] + scaled * terms[1, x, rows, :]))
        values.append(density * scal[2, x, rows, :])
        values.append(density * (scal[3, x, rows, :] + scaled * terms[2, x, rows, :]))
        values.append(density * scal[4, x, rows, :])
        for f, value in enumerate(values):
            cons[cycle, f, x + 1, pl.ds(PAD + y0, TILE), :] = value
        pack(cycle, 2, h, x, y0, values)
        pack_rows(cycle, 2, x, y0, values)

    present = jnp.zeros((1, nz), jnp.int32)
    block = lax.broadcasted_iota(jnp.int32, (1, nz), 1) // B
    for j in range(nz // B):
        value = mask_ref[index["gx"] * nx // B, index["gy"] * ny // B, index["gz"] * (nz // B) + j]
        present = jnp.where(block == j, value, present)

    def stage_remap(cycle, h, x, y0):
        rows = pl.ds(y0, TILE)
        active = jnp.broadcast_to(present, (TILE, nz)) > 0
        half_dt = 0.5 * step[0:1, :]
        velocity = [at(0, cycle, f, x, y0) for f in range(3)]
        z_ahead, z_behind = z_pair(cycle, 0, h, x, y0, 2, velocity[2])
        around = (
            (at(0, cycle, 0, x, y0, dx=1), at(0, cycle, 0, x, y0, dx=-1)),
            (at(0, cycle, 1, x, y0, dy=1), at(0, cycle, 1, x, y0, dy=-1)),
            (z_ahead, z_behind),
        )
        centre = 1.0
        into = []
        for j in range(3):
            upper = half_dt * (velocity[j] + around[j][0])
            lower = half_dt * (around[j][1] + velocity[j])
            up_in, down_in = jnp.minimum(upper, 0.0), jnp.maximum(lower, 0.0)
            centre = centre - (jnp.maximum(upper, 0.0) - jnp.minimum(lower, 0.0))
            into.append((up_in, down_in))

        def result(f):
            value = at(2, cycle, f, x, y0)
            ahead, behind = z_pair(cycle, 2, h, x, y0, f, value)
            return (
                centre * value
                - (into[0][0] * at(2, cycle, f, x, y0, dx=1) - into[0][1] * at(2, cycle, f, x, y0, dx=-1))
                - (into[1][0] * at(2, cycle, f, x, y0, dy=1) - into[1][1] * at(2, cycle, f, x, y0, dy=-1))
                - (into[2][0] * ahead - into[2][1] * behind)
            )

        density = result(0)
        inverse = 1.0 / density
        old = [scal[0, x, rows, :]] + velocity + [scal[n, x, rows, :] for n in range(1, 5)]
        new = [jnp.where(active, density, old[0])]
        for f in range(1, 8):
            new.append(jnp.where(active, result(f) * inverse, old[f]))
        if cycle == CYCLES - 1:
            for f in range(8):
                out_ref[f, x, rows, :] = new[f]
            return
        for n, f in enumerate((0, 4, 5, 6, 7)):
            scal[n, x, rows, :] = new[f]
        for f in range(3):
            vel[cycle + 1, f, x + 1, pl.ds(PAD + y0, TILE), :] = new[f + 1]
        inverse = jnp.where(active, inverse, inv[x, rows, :])
        inv[x, rows, :] = inverse
        begin(cycle + 1, h, x, y0, new[0], inverse, new[4], new[1:4])

    def peak_copy(cycle, phase, away):
        axis = AXES[2 - phase]
        return pltpu.make_async_remote_copy(
            src_ref=peak.at[cycle, phase, 0],
            dst_ref=peak.at[cycle, phase, away],
            send_sem=peak_send.at[cycle, phase, away],
            recv_sem=peak_recv.at[cycle, phase, away],
            device_id={axis: lax.rem(index[axis] + away, sizes[axis])},
            device_id_type=MESH,
        )

    def peak_send_all(cycle, phase):
        for away in range(1, sizes[AXES[2 - phase]]):
            peak_copy(cycle, phase, away).start()

    def peak_take(cycle, phase):
        top = peak[cycle, phase, 0]
        for away in range(1, sizes[AXES[2 - phase]]):
            peak_copy(cycle, phase, away).wait_recv()
            top = jnp.maximum(top, peak[cycle, phase, away])
        if phase < 2:
            peak[cycle, phase + 1, 0] = top
        else:
            fastest = jnp.max(jnp.max(top, axis=1, keepdims=True), axis=0, keepdims=True)
            step[...] = courant / jnp.broadcast_to(fastest, step.shape)

    for load in loads:
        load.wait()
    pl.semaphore_wait(barrier, total)

    for h in range(HALVES):
        planes(h, stage_start)
        send(0, 0, h)
    for cycle in range(CYCLES):
        peak_send_all(cycle, 0)
        for h in range(HALVES):
            receive(cycle, 0, h)
            planes(h, functools.partial(stage_stress, cycle))
            send(cycle, 1, h)
            peak_take(cycle, h)
            peak_send_all(cycle, h + 1)
        peak_take(cycle, 2)
        for h in range(HALVES):
            receive(cycle, 1, h)
            planes(h, functools.partial(stage_conserved, cycle))
            send(cycle, 2, h)
        for h in range(HALVES):
            receive(cycle, 2, h)
            planes(h, functools.partial(stage_remap, cycle))
            if cycle + 1 < CYCLES:
                send(cycle + 1, 0, h)

    for cycle in range(CYCLES):
        for phase in range(3):
            for away in range(1, sizes[AXES[2 - phase]]):
                peak_copy(cycle, phase, away).wait_send()
        for r in range(3):
            for s in range(2):
                way = above if s == 0 else below
                for_side(way["gx"], "gx", lambda: x_copy(cycle, r, s).wait_send())
                for h in range(HALVES):
                    for_side(way["gy"], "gy", lambda: y_copy(cycle, r, h, s).wait_send())
                    for_side(way["gz"], "gz", lambda: z_copy(cycle, r, h, s).wait_send())


def solution(mesh):
    sizes = {axis: mesh.shape[axis] for axis in AXES}

    def local(hydro_state, material_id, block_mask):
        _, nx, ny, nz = hydro_state.shape
        f32 = jnp.float32
        most = max(sizes.values())
        padded = (nx + 2, ny + 2 * PAD, nz)
        body = (nx, ny, nz)
        scratch = [
            pltpu.VMEM((CYCLES, 3) + padded, f32),
            pltpu.VMEM((CYCLES, 6) + padded, f32),
            pltpu.VMEM((CYCLES, 8) + padded, f32),
            pltpu.VMEM((5,) + body, f32),
            pltpu.VMEM(body, f32),
            pltpu.VMEM(body, jnp.int32),
            pltpu.VMEM(body, f32),
            pltpu.VMEM(body, f32),
            pltpu.VMEM((3,) + body, f32),
        ]
        for _ in range(2):
            scratch += [pltpu.VMEM((CYCLES, 2, count, nx, nz), f32) for count in COUNT]
        scratch += [
            pltpu.VMEM((CYCLES, 3, HALVES, ny, nz), f32),
            pltpu.VMEM((CYCLES, 3, HALVES, 2, ny, nz), f32),
            pltpu.VMEM((CYCLES, 3, HALVES, ny, nz), f32),
            pltpu.VMEM((CYCLES, 3, most, 8, nz), f32),
            pltpu.VMEM((8, nz), f32),
            pltpu.SemaphoreType.DMA((4,)),
            pltpu.SemaphoreType.DMA((CYCLES, 3, 2 + 4 * HALVES)),
            pltpu.SemaphoreType.DMA((CYCLES, 3, 2 + 4 * HALVES)),
            pltpu.SemaphoreType.DMA((CYCLES, 3, most)),
            pltpu.SemaphoreType.DMA((CYCLES, 3, most)),
        ]
        return pl.pallas_call(
            functools.partial(kernel, sizes),
            out_shape=jax.ShapeDtypeStruct(hydro_state.shape, f32),
            in_specs=[
                pl.BlockSpec(memory_space=pltpu.SMEM),
                pl.BlockSpec(memory_space=pl.ANY),
                pl.BlockSpec(memory_space=pl.ANY),
            ],
            out_specs=pl.BlockSpec(memory_space=pltpu.VMEM),
            scratch_shapes=scratch,
            compiler_params=pltpu.CompilerParams(
                collective_id=0, has_side_effects=True, vmem_limit_bytes=48 * 1024 * 1024
            ),
        )(block_mask, hydro_state, material_id)

    in_specs = (P(None, "gx", "gy", "gz"), P("gx", "gy", "gz"), P())
    out_specs = P(None, "gx", "gy", "gz")
    return jax.shard_map(local, mesh=mesh, in_specs=in_specs, out_specs=out_specs, check_vma=False)
```

profile of v0, /device:TPU:4, one launch (start us, length us, event | category | flops | bytes accessed | tf_op | source)
XLA Modules:
  0.0 51.8 jit_solution(17581295386700870034)
XLA Ops:
  0.0 0.0 copy-start
  0.0 1.6 %copy-done = f32[8,16,32,128]{3,2,1,0:T(8,128)S(1)} copy-done((f32[8,16,32,128]{3,2,1,0:T(8,128)S(1)}, f32[8,16,32,128]{3,2,1,0:T(8,128)}, u32[]{:S(2)}) %copy-start) | copy-done | bytes 2097176
  1.6 0.0 copy-start.1
  1.6 0.9 %copy-done.1 = s32[16,32,128]{2,1,0:T(8,128)S(1)} copy-done((s32[16,32,128]{2,1,0:T(8,128)S(1)}, s32[16,32,128]{2,1,0:T(8,128)}, u32[]{:S(2)}) %copy-start.1) | copy-done | bytes 262168
  2.5 0.0 copy-start.2
  2.5 0.7 %copy-done.2 = s32[1,4,16]{2,1,0:T(4,128)S(1)} copy-done((s32[1,4,16]{2,1,0:T(4,128)S(1)}, s32[1,4,16]{2,1,0:T(4,128)}, u32[]{:S(2)}) %copy-start.2) | copy-done | bytes 280
  3.2 47.3 %shard_map.37 = f32[8,16,32,128]{3,2,1,0:T(8,128)S(1)} custom-call(s32[1,4,16]{2,1,0:T(4,128)S(1)} %copy-done.2, f32[8,16,32,128]{3,2,1,0:T(8,128)S(1)} %copy-done, s32[16,32,128]{2,1,0:T(8,128)S(1)} %copy-done.1), custom_call_target="tpu_custom_call" | custom-call | tf_op jit(solution)/shard_map/pallas_call | solution.py:436
  50.5 1.3 %copy.5 = f32[8,16,32,128]{3,2,1,0:T(8,128)} copy(f32[8,16,32,128]{3,2,1,0:T(8,128)S(1)} %shard_map.37) | data formatting | bytes 4194304
Async XLA Ops:
  0.0 1.6 %copy-start = (f32[8,16,32,128]{3,2,1,0:T(8,128)S(1)}, f32[8,16,32,128]{3,2,1,0:T(8,128)}, u32[]{:S(2)}) copy-start(f32[8,16,32,128]{3,2,1,0:T(8,128)} %state_hbm.1) | copy-start | bytes 6291460
  1.6 0.9 %copy-start.1 = (s32[16,32,128]{2,1,0:T(8,128)S(1)}, s32[16,32,128]{2,1,0:T(8,128)}, u32[]{:S(2)}) copy-start(s32[16,32,128]{2,1,0:T(8,128)} %material_hbm.1) | copy-start | bytes 786436
  2.5 0.7 %copy-start.2 = (s32[1,4,16]{2,1,0:T(4,128)S(1)}, s32[1,4,16]{2,1,0:T(4,128)}, u32[]{:S(2)}) copy-start(s32[1,4,16]{2,1,0:T(4,128)} %mask_ref.1) | copy-start | bytes 772
where the time goes:
time: 52 us; the launch traced here: 51.8 us
  Pallas kernels  47.3 us (91%)
  local copies, waits for them, and re-layouts  4.54 us (9%)
    pallas_call x1, Pallas kernels, local(): pl.pallas_call(functools.partial(kernel, sizes), out_shape=jax.ShapeDtype...  47.3 us
    unnamed x7, local copies, waits for them, and re-layouts  4.54 us

commit v1 on v0

--- a/solution.py
+++ b/solution.py
@@ -13,6 +13,7 @@
 HALVES = 2
 PAD = 8
 TILE = 32
+GROUP = 2
 MESH = pl.DeviceIdType.MESH
 
 courant = 0.15
@@ -96,10 +97,6 @@
                         else:
                             zr[cycle, r, :, side] = jnp.zeros((HALVES, ny, nz), jnp.float32)
 
-    zs[...] = jnp.zeros_like(zs)
-    for cycle in range(CYCLES):
-        peak[cycle, 0, 0] = jnp.zeros((8, nz), jnp.float32)
-
     def copy(cycle, r, slot, side, src, dst, axis):
         move = 1 if side == 0 else sizes[axis] - 1
         return pltpu.make_async_remote_copy(
@@ -135,9 +132,15 @@
         if sizes[axis] > 1:
             pl.when(exists)(act)
 
+    def send_x(cycle, r, side):
+        for_side((above if side == 0 else below)["gx"], "gx", lambda: x_copy(cycle, r, side).start())
+
+    def receive_x(cycle, r, side):
+        for_side((below if side == 0 else above)["gx"], "gx", lambda: x_copy(cycle, r, side).wait_recv())
+
     def send(cycle, r, h):
-        side = 1 - h
-        for_side((above if side == 0 else below)["gx"], "gx", lambda: x_copy(cycle, r, side).start())
+        if h == 0:
+            send_x(cycle, r, 1)
         for s in range(2):
             way = above if s == 0 else below
             for_side(way["gy"], "gy", lambda: y_copy(cycle, r, h, s).start())
@@ -148,33 +151,29 @@
     pair = lane // 2
 
     def receive(cycle, r, h):
-        for_side((below if h == 0 else above)["gx"], "gx", lambda: x_copy(cycle, r, h).wait_recv())
+        if h == 1:
+            receive_x(cycle, r, 1)
         for s in range(2):
             way = below if s == 0 else above
             for_side(way["gy"], "gy", lambda: y_copy(cycle, r, h, s).wait_recv())
             for_side(way["gz"], "gz", lambda: z_copy(cycle, r, h, s).wait_recv())
         fields = STRESS[1] if r == 1 else range(COUNT[r])
 
-        def spread(i, carry):
-            x = h * half + i
+        for x in range(h * half, h * half + half):
             for n, f in enumerate(fields):
                 buffers[r][cycle, f, x + 1, pl.ds(PAD - 1, 1), :] = yr[r][cycle, 0, n, pl.ds(x, 1), :]
                 buffers[r][cycle, f, x + 1, pl.ds(PAD + ny, 1), :] = yr[r][cycle, 1, n, pl.ds(x, 1), :]
-            return carry
-
-        lax.fori_loop(0, half, spread, 0)
+
         odd = lax.broadcasted_iota(jnp.int32, (ny, nz), 1) % 2 == 1
         zc[cycle, r, h] = jnp.where(
             odd, pltpu.roll(zr[cycle, r, h, 0], 1, 1), pltpu.roll(zr[cycle, r, h, 1], nz - 1, 1)
         )
 
-    def pack(cycle, r, h, x, y0, values):
-        rows = pl.ds(y0, TILE)
-        edge = zs[cycle, r, h, rows, :]
+    def pack(h, x, edge, values):
         for n, value in enumerate(values):
             slot = (x - h * half) * len(values) + n
             edge = jnp.where(pair == slot, pltpu.roll(value, 2 * slot + 1, 1), edge)
-        zs[cycle, r, h, rows, :] = edge
+        return edge
 
     def pack_rows(cycle, r, x, y0, values):
         for n, value in enumerate(values):
@@ -193,36 +192,49 @@
         behind = jnp.where(first_lane, ghost, pltpu.roll(value, 1, 1))
         return ahead, behind
 
-    def planes(h, body):
+    def planes(h, body, cycle, gives, takes=None):
+        groups = half // GROUP
+
         def run(i, carry):
-            x = h * half + i
-            for y0 in range(0, ny, TILE):
-                body(h, x, y0)
-            return carry
-
-        lax.fori_loop(0, half, run, 0)
-
-    def begin(cycle, h, x, y0, density, inverse, energy, velocity):
+            edge, top = carry
+            if h == 0 and takes is not None:
+                pl.when(i == groups - 1)(lambda: receive_x(cycle, takes, 0))
+            for j in range(GROUP):
+                edge, top = body(h, (h + 1) * half - 1 - (i * GROUP + j), edge, top)
+            if h == 1 and gives is not None:
+                pl.when(i == 0)(lambda: send_x(gives[0], gives[1], 0))
+            return edge, top
+
+        init = (jnp.zeros((ny, nz), jnp.float32), jnp.zeros((8, nz), jnp.float32))
+        edge, top = lax.fori_loop(0, groups, run, init)
+        if gives is not None:
+            zs[gives[0], gives[1], h] = edge
+            if gives[1] == 0:
+                peak[gives[0], 0, 0] = top if h == 0 else jnp.maximum(peak[gives[0], 0, 0], top)
+            send(gives[0], gives[1], h)
+
+    def begin(cycle, h, x, edge, top, density, inverse, energy, velocity):
+        y0 = 0
         rows = pl.ds(y0, TILE)
         pressure, speed = equation_of_state(density, inverse, energy, mat[x, rows, :])
         pres[x, rows, :] = pressure
         sound[x, rows, :] = speed
         fast = speed + jnp.abs(velocity[0]) + jnp.abs(velocity[1]) + jnp.abs(velocity[2])
-        top = peak[cycle, 0, 0]
         for r0 in range(0, TILE, 8):
             top = jnp.maximum(top, fast[r0 : r0 + 8])
-        peak[cycle, 0, 0] = top
-        pack(cycle, 0, h, x, y0, velocity)
         pack_rows(cycle, 0, x, y0, velocity)
-
-    def stage_start(h, x, y0):
+        return pack(h, x, edge, velocity), top
+
+    def stage_start(h, x, edge, top):
+        y0 = 0
         rows = pl.ds(y0, TILE)
         density = scal[0, x, rows, :]
         inverse = 1.0 / density
         inv[x, rows, :] = inverse
-        begin(0, h, x, y0, density, inverse, scal[1, x, rows, :], [at(0, 0, f, x, y0) for f in range(3)])
-
-    def stage_stress(cycle, h, x, y0):
+        return begin(0, h, x, edge, top, density, inverse, scal[1, x, rows, :], [at(0, 0, f, x, y0) for f in range(3)])
+
+    def stage_stress(cycle, h, x, edge, top):
+        y0 = 0
         rows = pl.ds(y0, TILE)
         g = []
         for f in range(3):
@@ -252,10 +264,11 @@
         terms[0, x, rows, :] = div
         terms[1, x, rows, :] = heat - pressure * div
         terms[2, x, rows, :] = heat
-        pack(cycle, 1, h, x, y0, [values[f] for f in STRESS[2]])
         pack_rows(cycle, 1, x, y0, [values[f] for f in STRESS[1]])
-
-    def stage_conserved(cycle, h, x, y0):
+        return pack(h, x, edge, [values[f] for f in STRESS[2]]), top
+
+    def stage_conserved(cycle, h, x, edge, top):
+        y0 = 0
         rows = pl.ds(y0, TILE)
         dt = step[0:1, :]
         inverse = inv[x, rows, :]
@@ -277,8 +290,8 @@
         values.append(density * scal[4, x, rows, :])
         for f, value in enumerate(values):
             cons[cycle, f, x + 1, pl.ds(PAD + y0, TILE), :] = value
-        pack(cycle, 2, h, x, y0, values)
         pack_rows(cycle, 2, x, y0, values)
+        return pack(h, x, edge, values), top
 
     present = jnp.zeros((1, nz), jnp.int32)
     block = lax.broadcasted_iota(jnp.int32, (1, nz), 1) // B
@@ -286,7 +299,8 @@
         value = mask_ref[index["gx"] * nx // B, index["gy"] * ny // B, index["gz"] * (nz // B) + j]
         present = jnp.where(block == j, value, present)
 
-    def stage_remap(cycle, h, x, y0):
+    def stage_remap(cycle, h, x, edge, top):
+        y0 = 0
         rows = pl.ds(y0, TILE)
         active = jnp.broadcast_to(present, (TILE, nz)) > 0
         half_dt = 0.5 * step[0:1, :]
@@ -325,14 +339,14 @@
         if cycle == CYCLES - 1:
             for f in range(8):
                 out_ref[f, x, rows, :] = new[f]
-            return
+            return edge, top
         for n, f in enumerate((0, 4, 5, 6, 7)):
             scal[n, x, rows, :] = new[f]
         for f in range(3):
             vel[cycle + 1, f, x + 1, pl.ds(PAD + y0, TILE), :] = new[f + 1]
         inverse = jnp.where(active, inverse, inv[x, rows, :])
         inv[x, rows, :] = inverse
-        begin(cycle + 1, h, x, y0, new[0], inverse, new[4], new[1:4])
+        return begin(cycle + 1, h, x, edge, top, new[0], inverse, new[4], new[1:4])
 
     def peak_copy(cycle, phase, away):
         axis = AXES[2 - phase]
@@ -365,26 +379,22 @@
     pl.semaphore_wait(barrier, total)
 
     for h in range(HALVES):
-        planes(h, stage_start)
-        send(0, 0, h)
+        planes(h, stage_start, 0, (0, 0))
     for cycle in range(CYCLES):
         peak_send_all(cycle, 0)
         for h in range(HALVES):
             receive(cycle, 0, h)
-            planes(h, functools.partial(stage_stress, cycle))
-            send(cycle, 1, h)
+            planes(h, functools.partial(stage_stress, cycle), cycle, (cycle, 1), 0)
             peak_take(cycle, h)
             peak_send_all(cycle, h + 1)
         peak_take(cycle, 2)
         for h in range(HALVES):
             receive(cycle, 1, h)
-            planes(h, functools.partial(stage_conserved, cycle))
-            send(cycle, 2, h)
+            planes(h, functools.partial(stage_conserved, cycle), cycle, (cycle, 2), 1)
         for h in range(HALVES):
             receive(cycle, 2, h)
-            planes(h, functools.partial(stage_remap, cycle))
-            if cycle + 1 < CYCLES:
-                send(cycle + 1, 0, h)
+            after = (cycle + 1, 0) if cycle + 1 < CYCLES else None
+            planes(h, functools.partial(stage_remap, cycle), cycle, after, 2)
 
     for cycle in range(CYCLES):
         for phase in range(3):

time: 52 us -> 46.9 us (0.902)
  the two profiles are of different devices: /device:TPU:4 before, /device:TPU:1 now
where the time goes in v1:
time: 46.9 us; the launch traced here: 46.7 us
  Pallas kernels  42.1 us (90%)
  local copies, waits for them, and re-layouts  4.54 us (10%)
    pallas_call x1, Pallas kernels, local(): pl.pallas_call(functools.partial(kernel, sizes), out_shape=jax.ShapeDtype...  42.1 us
    unnamed x7, local copies, waits for them, and re-layouts  4.54 us

profile of v1, /device:TPU:1, one launch (start us, length us, event | category | flops | bytes accessed | tf_op | source)
XLA Modules:
  0.0 46.7 jit_solution(12407720534496269756)
XLA Ops:
  0.0 0.0 copy-start
  0.0 1.6 %copy-done = f32[8,16,32,128]{3,2,1,0:T(8,128)S(1)} copy-done((f32[8,16,32,128]{3,2,1,0:T(8,128)S(1)}, f32[8,16,32,128]{3,2,1,0:T(8,128)}, u32[]{:S(2)}) %copy-start) | copy-done | bytes 2097176
  1.6 0.0 copy-start.1
  1.6 0.9 %copy-done.1 = s32[16,32,128]{2,1,0:T(8,128)S(1)} copy-done((s32[16,32,128]{2,1,0:T(8,128)S(1)}, s32[16,32,128]{2,1,0:T(8,128)}, u32[]{:S(2)}) %copy-start.1) | copy-done | bytes 262168
  2.5 0.0 copy-start.2
  2.5 0.7 %copy-done.2 = s32[1,4,16]{2,1,0:T(4,128)S(1)} copy-done((s32[1,4,16]{2,1,0:T(4,128)S(1)}, s32[1,4,16]{2,1,0:T(4,128)}, u32[]{:S(2)}) %copy-start.2) | copy-done | bytes 280
  3.2 42.1 %shard_map.37 = f32[8,16,32,128]{3,2,1,0:T(8,128)S(1)} custom-call(s32[1,4,16]{2,1,0:T(4,128)S(1)} %copy-done.2, f32[8,16,32,128]{3,2,1,0:T(8,128)S(1)} %copy-done, s32[16,32,128]{2,1,0:T(8,128)S(1)} %copy-done.1), custom_call_target="tpu_custom_call" | custom-call | tf_op jit(solution)/shard_map/pallas_call | solution.py:446
  45.3 1.3 %copy.5 = f32[8,16,32,128]{3,2,1,0:T(8,128)} copy(f32[8,16,32,128]{3,2,1,0:T(8,128)S(1)} %shard_map.37) | data formatting | bytes 4194304
Async XLA Ops:
  0.0 1.6 %copy-start = (f32[8,16,32,128]{3,2,1,0:T(8,128)S(1)}, f32[8,16,32,128]{3,2,1,0:T(8,128)}, u32[]{:S(2)}) copy-start(f32[8,16,32,128]{3,2,1,0:T(8,128)} %state_hbm.1) | copy-start | bytes 6291460
  1.6 0.9 %copy-start.1 = (s32[16,32,128]{2,1,0:T(8,128)S(1)}, s32[16,32,128]{2,1,0:T(8,128)}, u32[]{:S(2)}) copy-start(s32[16,32,128]{2,1,0:T(8,128)} %material_hbm.1) | copy-start | bytes 786436
  2.5 0.7 %copy-start.2 = (s32[1,4,16]{2,1,0:T(4,128)S(1)}, s32[1,4,16]{2,1,0:T(4,128)}, u32[]{:S(2)}) copy-start(s32[1,4,16]{2,1,0:T(4,128)} %mask_ref.1) | copy-start | bytes 772

commit v2 on v1

--- a/solution.py
+++ b/solution.py
@@ -73,12 +73,19 @@
     for load in loads:
         load.start()
 
+    peers = (sizes["gz"], sizes["gx"] * sizes["gy"])
+
+    def peer_at(phase, away):
+        if phase == 0:
+            return {"gz": lax.rem(index["gz"] + away, peers[0])}
+        place = lax.rem(index["gx"] * sizes["gy"] + index["gy"] + away, peers[1])
+        return {"gx": place // sizes["gy"], "gy": lax.rem(place, sizes["gy"])}
+
     barrier = pltpu.get_barrier_semaphore()
     total = 0
-    for axis in AXES:
-        for away in range(1, sizes[axis]):
-            peer = lax.rem(index[axis] + away, sizes[axis])
-            pl.semaphore_signal(barrier, inc=1, device_id={axis: peer}, device_id_type=MESH)
+    for phase in range(2):
+        for away in range(1, peers[phase]):
+            pl.semaphore_signal(barrier, inc=1, device_id=peer_at(phase, away), device_id_type=MESH)
             total += 1
 
     for axis_number, axis in enumerate(AXES):
@@ -349,26 +356,25 @@
         return begin(cycle + 1, h, x, edge, top, new[0], inverse, new[4], new[1:4])
 
     def peak_copy(cycle, phase, away):
-        axis = AXES[2 - phase]
         return pltpu.make_async_remote_copy(
             src_ref=peak.at[cycle, phase, 0],
             dst_ref=peak.at[cycle, phase, away],
             send_sem=peak_send.at[cycle, phase, away],
             recv_sem=peak_recv.at[cycle, phase, away],
-            device_id={axis: lax.rem(index[axis] + away, sizes[axis])},
+            device_id=peer_at(phase, away),
             device_id_type=MESH,
         )
 
     def peak_send_all(cycle, phase):
-        for away in range(1, sizes[AXES[2 - phase]]):
+        for away in range(1, peers[phase]):
             peak_copy(cycle, phase, away).start()
 
     def peak_take(cycle, phase):
         top = peak[cycle, phase, 0]
-        for away in range(1, sizes[AXES[2 - phase]]):
+        for away in range(1, peers[phase]):
             peak_copy(cycle, phase, away).wait_recv()
             top = jnp.maximum(top, peak[cycle, phase, away])
-        if phase < 2:
+        if phase < 1:
             peak[cycle, phase + 1, 0] = top
         else:
             fastest = jnp.max(jnp.max(top, axis=1, keepdims=True), axis=0, keepdims=True)
@@ -385,11 +391,13 @@
         for h in range(HALVES):
             receive(cycle, 0, h)
             planes(h, functools.partial(stage_stress, cycle), cycle, (cycle, 1), 0)
-            peak_take(cycle, h)
-            peak_send_all(cycle, h + 1)
-        peak_take(cycle, 2)
+            if h == 0:
+                peak_take(cycle, 0)
+                peak_send_all(cycle, 1)
         for h in range(HALVES):
             receive(cycle, 1, h)
+            if h == 0:
+                peak_take(cycle, 1)
             planes(h, functools.partial(stage_conserved, cycle), cycle, (cycle, 2), 1)
         for h in range(HALVES):
             receive(cycle, 2, h)
@@ -397,8 +405,8 @@
             planes(h, functools.partial(stage_remap, cycle), cycle, after, 2)
 
     for cycle in range(CYCLES):
-        for phase in range(3):
-            for away in range(1, sizes[AXES[2 - phase]]):
+        for phase in range(2):
+            for away in range(1, peers[phase]):
                 peak_copy(cycle, phase, away).wait_send()
         for r in range(3):
             for s in range(2):
@@ -415,7 +423,7 @@
     def local(hydro_state, material_id, block_mask):
         _, nx, ny, nz = hydro_state.shape
         f32 = jnp.float32
-        most = max(sizes.values())
+        most = max(sizes["gz"], sizes["gx"] * sizes["gy"])
         padded = (nx + 2, ny + 2 * PAD, nz)
         body = (nx, ny, nz)
         scratch = [
@@ -435,13 +443,13 @@
             pltpu.VMEM((CYCLES, 3, HALVES, ny, nz), f32),
             pltpu.VMEM((CYCLES, 3, HALVES, 2, ny, nz), f32),
             pltpu.VMEM((CYCLES, 3, HALVES, ny, nz), f32),
-            pltpu.VMEM((CYCLES, 3, most, 8, nz), f32),
+            pltpu.VMEM((CYCLES, 2, most, 8, nz), f32),
             pltpu.VMEM((8, nz), f32),
             pltpu.SemaphoreType.DMA((4,)),
             pltpu.SemaphoreType.DMA((CYCLES, 3, 2 + 4 * HALVES)),
             pltpu.SemaphoreType.DMA((CYCLES, 3, 2 + 4 * HALVES)),
-            pltpu.SemaphoreType.DMA((CYCLES, 3, most)),
-            pltpu.SemaphoreType.DMA((CYCLES, 3, most)),
+            pltpu.SemaphoreType.DMA((CYCLES, 2, most)),
+            pltpu.SemaphoreType.DMA((CYCLES, 2, most)),
         ]
         return pl.pallas_call(
             functools.partial(kernel, sizes),

time: 46.9 us -> 43.4 us (0.925)
  Pallas kernels: 42.1 us -> 38.7 us
    pallas_call x1, Pallas kernels: 42.1 us -> 38.7 us  [local(): pl.pallas_call(functools.partial(kernel, sizes), out_shape=jax.ShapeDtype...]
where the time goes in v2:
time: 43.4 us; the launch traced here: 43.3 us
  Pallas kernels  38.7 us (89%)
  local copies, waits for them, and re-layouts  4.54 us (10%)
    pallas_call x1, Pallas kernels, local(): pl.pallas_call(functools.partial(kernel, sizes), out_shape=jax.ShapeDtype...  38.7 us
    unnamed x7, local copies, waits for them, and re-layouts  4.54 us

profile of v2, /device:TPU:1, one launch (start us, length us, event | category | flops | bytes accessed | tf_op | source)
XLA Modules:
  0.0 43.3 jit_solution(2061353689256319311)
XLA Ops:
  0.0 0.0 copy-start
  0.0 1.6 %copy-done = f32[8,16,32,128]{3,2,1,0:T(8,128)S(1)} copy-done((f32[8,16,32,128]{3,2,1,0:T(8,128)S(1)}, f32[8,16,32,128]{3,2,1,0:T(8,128)}, u32[]{:S(2)}) %copy-start) | copy-done | bytes 2097176
  1.6 0.0 copy-start.1
  1.6 0.9 %copy-done.1 = s32[16,32,128]{2,1,0:T(8,128)S(1)} copy-done((s32[16,32,128]{2,1,0:T(8,128)S(1)}, s32[16,32,128]{2,1,0:T(8,128)}, u32[]{:S(2)}) %copy-start.1) | copy-done | bytes 262168
  2.5 0.0 copy-start.2
  2.5 0.7 %copy-done.2 = s32[1,4,16]{2,1,0:T(4,128)S(1)} copy-done((s32[1,4,16]{2,1,0:T(4,128)S(1)}, s32[1,4,16]{2,1,0:T(4,128)}, u32[]{:S(2)}) %copy-start.2) | copy-done | bytes 280
  3.2 38.7 %shard_map.37 = f32[8,16,32,128]{3,2,1,0:T(8,128)S(1)} custom-call(s32[1,4,16]{2,1,0:T(4,128)S(1)} %copy-done.2, f32[8,16,32,128]{3,2,1,0:T(8,128)S(1)} %copy-done, s32[16,32,128]{2,1,0:T(8,128)S(1)} %copy-done.1), custom_call_target="tpu_custom_call" | custom-call | tf_op jit(solution)/shard_map/pallas_call | solution.py:454
  41.9 1.3 %copy.5 = f32[8,16,32,128]{3,2,1,0:T(8,128)} copy(f32[8,16,32,128]{3,2,1,0:T(8,128)S(1)} %shard_map.37) | data formatting | bytes 4194304
Async XLA Ops:
  0.0 1.6 %copy-start = (f32[8,16,32,128]{3,2,1,0:T(8,128)S(1)}, f32[8,16,32,128]{3,2,1,0:T(8,128)}, u32[]{:S(2)}) copy-start(f32[8,16,32,128]{3,2,1,0:T(8,128)} %state_hbm.1) | copy-start | bytes 6291460
  1.6 0.9 %copy-start.1 = (s32[16,32,128]{2,1,0:T(8,128)S(1)}, s32[16,32,128]{2,1,0:T(8,128)}, u32[]{:S(2)}) copy-start(s32[16,32,128]{2,1,0:T(8,128)} %material_hbm.1) | copy-start | bytes 786436
  2.5 0.7 %copy-start.2 = (s32[1,4,16]{2,1,0:T(4,128)S(1)}, s32[1,4,16]{2,1,0:T(4,128)}, u32[]{:S(2)}) copy-start(s32[1,4,16]{2,1,0:T(4,128)} %mask_ref.1) | copy-start | bytes 772
